TPU v7x, 32 devices: a whole 2x2x4 slice. The times are simulated.
32 devices in a mesh: row: 8 (over y, x, core), col: 4 (over z).
Axes of the slice: x: 2, y: 2, z: 4, core: 2. Of those that a mesh axis runs over, the one named last changes fastest.
Arguments:
- amplitudes: bfloat16 [7168, 7168], P('row', 'col'), as said below
- integrals: bfloat16 [7168, 7168], P('row', 'col'), as said below
- occ_energy: float32 [80], replicated, may hold values from -2 to -0.5
- vir_energy: float32 [1000], replicated, may hold values from 0.5 to 4
- pair_occ: int32 [7168], replicated, may hold values from 0 to 79, as said below
- pair_vir: int32 [7168], replicated, may hold values from 0 to 999, as said below
Outputs:
- updated: float32 [7168, 7168], P('row', 'col')
Inputs may be any that keep to these rules, and one draw needn't show every extreme that they name: amplitudes is exactly symmetric. integrals is exactly symmetric. pair_occ[p] mod 8 equals pair_vir[p] mod 8 (one irrep block), and no pair (pair_occ[p], pair_vir[p]) occurs twice. `pair_vir`: see pair_occ.
All inputs are finite; a program needn't handle non-finite values.
Results may differ from a plain program's by a relative error of at most 0.0003.
Values may be sent and summed in bfloat16 or wider, within the bound.
A program may use at most 192 MiB of HBM per device.

v0:
```python
import jax
import jax.numpy as jnp
from jax import lax
from jax.sharding import PartitionSpec as P


def lookup(energies, orbital_index):
    labels = jnp.arange(energies.shape[0], dtype=jnp.int32)
    picked = jnp.where(orbital_index[:, None] == labels[None, :], energies[None, :], 0.0)
    return jnp.sum(picked, axis=1)


def shards(amplitudes, integrals, occ_energy, vir_energy, pair_occ, pair_vir):
    tile_rows, tile_cols = amplitudes.shape
    left_local = jnp.stack((amplitudes, integrals))
    right_local = jnp.stack((integrals, amplitudes))
    row_panels = lax.all_gather(left_local, "col", axis=2, tiled=True)
    summed = jnp.einsum(
        "lrk,lkc->rc",
        row_panels,
        lax.all_gather(right_local, "row", axis=1, tiled=True),
        preferred_element_type=jnp.float32,
    )
    row_start = lax.axis_index("row") * tile_rows
    col_start = lax.axis_index("col") * tile_cols
    row_occ = lax.dynamic_slice_in_dim(pair_occ, row_start, tile_rows)
    row_vir = lax.dynamic_slice_in_dim(pair_vir, row_start, tile_rows)
    col_occ = lax.dynamic_slice_in_dim(pair_occ, col_start, tile_cols)
    col_vir = lax.dynamic_slice_in_dim(pair_vir, col_start, tile_cols)
    row_gap = lookup(occ_energy, row_occ) - lookup(vir_energy, row_vir)
    col_gap = lookup(occ_energy, col_occ) - lookup(vir_energy, col_vir)
    return summed / (row_gap[:, None] + col_gap[None, :])


def solution(mesh):
    return jax.shard_map(
        shards,
        mesh=mesh,
        in_specs=(P("row", "col"), P("row", "col"), P(), P(), P(), P()),
        out_specs=P("row", "col"),
        check_vma=False,
    )
```

profile of v0, /device:TPU:0, one launch (start us, length us, event | category | flops | bytes accessed | tf_op | source)
XLA Modules:
  0.0 753.5 jit_solution(10933754209903667477)
XLA Ops:
  6.5 0.0 all-gather.3.cloned.1.call-start
  6.5 11.5 %pad_maximum_fusion.1 = (bf16[2,896,1792]{2,1,0:T(8,128)(2,1)}, bf16[2,896,1792]{2,1,0:T(8,128)(2,1)}) fusion(bf16[1,896,1792]{2,1,0:T(8,128)(2,1)} %bitcast.6, bf16[1,896,1792]{2,1,0:T(8,128)(2,1)} %bitcast.7), kind=kLoop, calls=%fused_computation.3 | loop fusion | flops 6422528 | bytes 19267584 | tf_op jit(solution)/shard_map/stack | solution.py:16
  18.1 0.0 copy-start.1
  18.1 0.0 copy-start
  18.1 0.0 all-gather.3.cloned.1.call-update
  18.1 0.0 all-gather.5.cloned.1.call-start
  18.2 0.7 all-gather.5.cloned.1.call-update
  18.9 0.8 dynamic_slice.14
  19.7 0.8 dynamic_slice.15
  20.4 0.8 dynamic_slice.12
  21.2 0.8 dynamic_slice.13
  22.0 0.0 copy-done.1
  22.0 0.2 select_reduce_fusion.2
  22.1 0.0 copy-done
  22.2 0.9 select_reduce_fusion
  23.0 0.1 select_reduce_fusion.3
  23.2 0.5 select_reduce_fusion.1
  23.6 431.0 %all-gather.3.cloned.1.call-done = bf16[2,896,7168]{2,1,0:T(8,128)(2,1)} async-done(((bf16[2,896,1792]{2,1,0:T(8,128)(2,1)}), bf16[2,896,7168]{2,1,0:T(8,128)(2,1)}) %all-gather.3.cloned.1.call-update) | async-done | bytes 25690128 | tf_op jit(solution)/shard_map/all_gather | solution.py:17
  454.6 236.4 %all-gather.5.cloned.1.call-done = bf16[2,7168,1792]{2,1,0:T(8,128)(2,1)} async-done(((bf16[2,896,1792]{2,1,0:T(8,128)(2,1)}), bf16[2,7168,1792]{2,1,0:T(8,128)(2,1)}) %all-gather.5.cloned.1.call-update) | async-done | bytes 51380240 | tf_op jit(solution)/shard_map/all_gather | solution.py:21
  691.0 55.6 %bitcast_divide_fusion = f32[896,1792]{1,0:T(8,128)} fusion(bf16[2,896,7168]{2,1,0:T(8,128)(2,1)} %all-gather.3.cloned.1.call-done, bf16[2,7168,1792]{2,1,0:T(8,128)(2,1)} %all-gather.5.cloned.1.call-done, f32[1792]{0:T(1024)S(1)} %sub.15, f32[896]{0:T(1024)S(1)} %sub.14), kind=kOutput, calls=%fused_computation.4 | convolution fusion | flops 46039891968 | bytes 83503616 | tf_op jit(solution)/shard_map/lrk,lkc->rc/dot_general | solution.py:18
  (2 shorter events, 0.0 us)
Async XLA Ops:
  6.5 448.1 %all-gather.3.cloned.1.call-start = ((), (), s32[]{:S(2)}) async-start(), calls=%async_computation | async-start | bytes 32112640 | tf_op jit(solution)/shard_map/all_gather | solution.py:17
  18.1 3.9 copy-start.1
  18.1 4.1 copy-start
  18.1 672.9 %all-gather.5.cloned.1.call-start = ((), (), s32[]{:S(2)}) async-start(), calls=%async_computation.1 | async-start | bytes 57802752 | tf_op jit(solution)/shard_map/all_gather | solution.py:21
Sparse Core Ops, SparseCore 0:
  18.2 436.3 all-gather.2
  456.5 234.4 all-gather.4
where the time goes:
time: 754 us
  waiting for transfers between devices  668 us (89%)
  matrix products  55.6 us (7%)
  between operations  13.5 us (2%)
  other arithmetic  13.2 us (2%)
    all_gather x1, waiting for transfers between devices, shards(): row_panels = lax.all_gather(left_local, 'col', axis=2, tiled=True)  431 us
    all_gather x1, waiting for transfers between devices, shards(): lax.all_gather(right_local, 'row', axis=1, tiled=True)  236 us
    dot_general x1, matrix products, shards(): jnp.einsum('lrk,lkc->rc', row_panels, lax.all_gather(right_local, 'row',...  55.6 us
  transfers between devices with their start and end apart: 2, of which 2 were waited for; matrix products, arithmetic and copies ran while one was open for 1% of the time, Pallas kernels for 0%

commit v1 on v0

v1 whole, which is shorter than its diff:
```python
import jax
import jax.numpy as jnp
from jax import lax
from jax.sharding import PartitionSpec as P


def lookup(energies, orbital_index):
    labels = jnp.arange(energies.shape[0], dtype=jnp.int32)
    picked = jnp.where(orbital_index[:, None] == labels[None, :], energies[None, :], 0.0)
    return jnp.sum(picked, axis=1)


def arrivals(col, cols):
    order = []
    for hops in range(1, cols):
        if col >= hops:
            order.append((0, hops))
        if col + hops < cols:
            order.append((1, hops))
    return order


def chains(block, cols):
    held = {}
    up = down = block
    for hops in range(1, cols):
        up = lax.ppermute(up, "col", [(c, c + 1) for c in range(hops - 1, cols - 1)])
        down = lax.ppermute(down, "col", [(c, c - 1) for c in range(1, cols - hops + 1)])
        held[0, hops], held[1, hops] = up, down
    return held


def choose(held, sources, col):
    kinds = sorted(set(sources))
    picked = held[kinds[0]]
    for kind in kinds[1:]:
        wanted = jnp.zeros((), bool)
        for c, source in enumerate(sources):
            if source == kind:
                wanted = wanted | (col == c)
        picked = jnp.where(wanted, held[kind], picked)
    return picked


def shards_of(cols):
    orders = [arrivals(c, cols) for c in range(cols)]

    def shards(amplitudes, integrals, occ_energy, vir_energy, pair_occ, pair_vir):
        tile_rows, tile_cols = amplitudes.shape
        row, col = lax.axis_index("row"), lax.axis_index("col")
        amp_held = chains(amplitudes, cols)
        int_held = chains(integrals, cols)
        amp_panel = lax.all_gather(amplitudes, "row", axis=0, tiled=True)
        int_panel = lax.all_gather(integrals, "row", axis=0, tiled=True)

        row_occ = lax.dynamic_slice_in_dim(pair_occ, row * tile_rows, tile_rows)
        row_vir = lax.dynamic_slice_in_dim(pair_vir, row * tile_rows, tile_rows)
        col_occ = lax.dynamic_slice_in_dim(pair_occ, col * tile_cols, tile_cols)
        col_vir = lax.dynamic_slice_in_dim(pair_vir, col * tile_cols, tile_cols)
        row_gap = lookup(occ_energy, row_occ) - lookup(vir_energy, row_vir)
        col_gap = lookup(occ_energy, col_occ) - lookup(vir_energy, col_vir)

        def term(amp, integ, k):
            int_block = lax.dynamic_slice_in_dim(int_panel, k * tile_cols, tile_cols)
            amp_block = lax.dynamic_slice_in_dim(amp_panel, k * tile_cols, tile_cols)
            return jnp.dot(amp, int_block, preferred_element_type=jnp.float32) + jnp.dot(
                integ, amp_block, preferred_element_type=jnp.float32
            )

        total = term(amplitudes, integrals, col)
        for slot in range(cols - 1):
            sources = [order[slot] for order in orders]
            k = jnp.zeros((), jnp.int32)
            for c, (direction, hops) in enumerate(sources):
                k = jnp.where(col == c, c + hops if direction else c - hops, k)
            total = total + term(
                choose(amp_held, sources, col), choose(int_held, sources, col), k
            )
        return total / (row_gap[:, None] + col_gap[None, :])

    return shards


def solution(mesh):
    return jax.shard_map(
        shards_of(mesh.shape["col"]),
        mesh=mesh,
        in_specs=(P("row", "col"), P("row", "col"), P(), P(), P(), P()),
        out_specs=P("row", "col"),
        check_vma=False,
    )
```

time: 754 us -> 467 us (0.62)
  waiting for transfers between devices: 668 us -> 302 us
  matrix products: 55.6 us -> 106 us
  starting transfers between devices: 0.04 us -> 30.7 us
  other arithmetic: 13.2 us -> 1.61 us
  local copies, waits for them, and re-layouts: 3.12 us -> 11.3 us
    all_gather x2, waiting for transfers between devices: 667 us -> 0.01 us  [the longest x1 0.01 us: shards(): amp_panel = lax.all_gather(amplitudes, 'row', axis=0, tiled=True)]
    ppermute x0 -> x12, waiting for transfers between devices: none -> 300 us  [the longest x6 300 us: chains(): lax.ppermute(down, 'col', [(c, c - 1) for c in range(1, cols - hops + 1)])]
    dot_general x1 -> x8, matrix products: 55.6 us -> 106 us  [the longest x4 58.4 us: term(): jnp.dot(amp, int_block, preferred_element_type=jnp.float32)]
    ppermute x0 -> x12, starting transfers between devices: none -> 30.7 us  [the longest x6 23 us: chains(): lax.ppermute(up, 'col', [(c, c + 1) for c in range(hops - 1, cols - 1)])]
    another operation x1 -> x0, other arithmetic: 11.5 us -> none  [shards(): right_local = jnp.stack((integrals, amplitudes))]
    div x0 -> x1, local copies, waits for them, and re-layouts: none -> 7.76 us  [shards(): return total / (row_gap[:, None] + col_gap[None, :])]
  transfers between devices with their start and end apart: 2 -> 14, of which waited for: 2 -> 7; matrix products, arithmetic and copies ran while one was open for 1% -> 19% of each run, Pallas kernels for 0% -> 0%
where the time goes in v1:
time: 467 us; the launch traced here: 465 us
  waiting for transfers between devices  302 us (65%)
  matrix products  106 us (23%)
  starting transfers between devices  30.7 us (7%)
  between operations  13.5 us (3%)
  local copies, waits for them, and re-layouts  11.3 us (2%)
    ppermute x6, waiting for transfers between devices, chains(): lax.ppermute(down, 'col', [(c, c - 1) for c in range(1, cols - hops + 1)])  300 us
    dot_general x4, matrix products, term(): jnp.dot(amp, int_block, preferred_element_type=jnp.float32)  58.4 us
    dot_general x4, matrix products, term(): jnp.dot(integ, amp_block, preferred_element_type=jnp.float32)  47.7 us
    ppermute x6, starting transfers between devices, chains(): lax.ppermute(up, 'col', [(c, c + 1) for c in range(hops - 1, cols - 1)])  23 us
  transfers between devices with their start and end apart: 14, of which 7 were waited for; matrix products, arithmetic and copies ran while one was open for 19% of the time, Pallas kernels for 0%

profile of v1, /device:TPU:0, one launch (start us, length us, event | category | flops | bytes accessed | tf_op | source)
XLA Modules:
  0.0 464.9 jit_solution(11964295174744376406)
XLA Ops:
  6.5 0.0 all-gather.5.cloned.1.call-start
  6.5 0.7 all-gather.5.cloned.1.call-update
  7.3 0.0 all-gather.3.cloned.1.call-start
  7.3 0.7 all-gather.3.cloned.1.call-update
  8.0 0.4 copy-done
  8.4 1.3 collective-permute-start.2
  9.7 7.3 %collective-permute-start.3 = (bf16[896,1792]{1,0:T(8,128)(2,1)S(1)}, bf16[896,1792]{1,0:T(8,128)(2,1)}, u32[]{:S(2)}, u32[]{:S(2)}) collective-permute-start(bf16[896,1792]{1,0:T(8,128)(2,1)S(1)} %copy-done), channel_id=1, source_target_pairs={{0,1},{1,2},{2,3},{4,5},{5,6},{6,7},{8,9},{9,10},{10,11},{12,13},{... | collective-permute-start | bytes 9633800 | tf_op jit(solution)/shard_map/ppermute | solution.py:27
  17.0 1.3 collective-permute-start
  18.3 6.3 %collective-permute-start.1 = (bf16[896,1792]{1,0:T(8,128)(2,1)}, bf16[896,1792]{1,0:T(8,128)(2,1)}, u32[]{:S(2)}, u32[]{:S(2)}) collective-permute-start(bf16[896,1792]{1,0:T(8,128)(2,1)} %param.6), channel_id=1, source_target_pairs={{0,1},{1,2},{2,3},{4,5},{5,6},{6,7},{8,9},{9,10},{10,11},{12,13},{... | collective-permute-start | bytes 9633800 | tf_op jit(solution)/shard_map/ppermute | solution.py:27
  24.6 59.2 %collective-permute-done.2 = bf16[896,1792]{1,0:T(8,128)(2,1)} collective-permute-done((bf16[896,1792]{1,0:T(8,128)(2,1)S(1)}, bf16[896,1792]{1,0:T(8,128)(2,1)}, u32[]{:S(2)}, u32[]{:S(2)}) %collective-permute-start.2) | collective-permute-done | bytes 3211296 | tf_op jit(solution)/shard_map/ppermute | solution.py:28
  83.8 1.3 collective-permute-start.6
  85.1 0.1 collective-permute-done.3
  85.2 2.3 collective-permute-start.7
  87.5 65.1 %collective-permute-done = bf16[896,1792]{1,0:T(8,128)(2,1)} collective-permute-done((bf16[896,1792]{1,0:T(8,128)(2,1)}, bf16[896,1792]{1,0:T(8,128)(2,1)}, u32[]{:S(2)}, u32[]{:S(2)}) %collective-permute-start) | collective-permute-done | bytes 3211296 | tf_op jit(solution)/shard_map/ppermute | solution.py:28
  152.6 1.3 collective-permute-start.4
  153.9 0.0 collective-permute-done.1
  153.9 2.3 collective-permute-start.5
  156.2 0.8 dynamic_slice.47
  157.0 0.8 dynamic_slice.46
  157.8 0.8 dynamic_slice.45
  158.6 0.8 dynamic_slice.44
  159.3 0.0 copy-done.3
  159.3 0.2 select_reduce_fusion.2
  159.5 0.0 copy-done.2
  159.5 0.9 select_reduce_fusion
  160.4 0.1 select_reduce_fusion.3
  160.5 0.5 select_reduce_fusion.1
  161.0 60.4 %collective-permute-done.6 = bf16[896,1792]{1,0:T(8,128)(2,1)} collective-permute-done((bf16[896,1792]{1,0:T(8,128)(2,1)}, bf16[896,1792]{1,0:T(8,128)(2,1)}, u32[]{:S(2)}, u32[]{:S(2)}) %collective-permute-start.6) | collective-permute-done | bytes 3211296 | tf_op jit(solution)/shard_map/ppermute | solution.py:28
  221.4 1.3 collective-permute-start.10
  222.7 0.0 collective-permute-done.7
  222.7 2.4 collective-permute-start.11
  225.2 65.1 %collective-permute-done.4 = bf16[896,1792]{1,0:T(8,128)(2,1)} collective-permute-done((bf16[896,1792]{1,0:T(8,128)(2,1)}, bf16[896,1792]{1,0:T(8,128)(2,1)}, u32[]{:S(2)}, u32[]{:S(2)}) %collective-permute-start.4) | collective-permute-done | bytes 3211296 | tf_op jit(solution)/shard_map/ppermute | solution.py:28
  290.2 1.3 collective-permute-start.8
  291.5 0.0 collective-permute-done.5
  291.5 2.3 collective-permute-start.9
  293.9 12.6 %fusion.7 = f32[896,1792]{0,1:T(8,128)} fusion(bf16[7168,1792]{1,0:T(8,128)(2,1)} %all-gather.5.cloned.1.call-done, s32[]{:T(128)S(6)} %select_n.149, bf16[896,1792]{1,0:T(8,128)(2,1)} %collective-permute-done.6, bf16[896,1792]{1,0:T(8,128)(2,1)} %collective-permute-done.2, bf16[896,1792]{1,0:T(8,128)(2,1)} %collective-permute-done.7, pred[]{:T(512)S(6)} %or.4, ...), kind=kOutput, calls=%fused_computation.10 | convolution fusion | flops 5757796352 | bytes 22478854 | tf_op jit(solution)/shard_map/dot_general | solution.py:66
  306.5 12.6 %fusion.9 = f32[896,1792]{0,1:T(8,128)} fusion(bf16[7168,1792]{1,0:T(8,128)(2,1)} %all-gather.3.cloned.1.call-done, s32[]{:T(128)S(6)} %select_n.149, bf16[896,1792]{1,0:T(8,128)(2,1)} %collective-permute-done.4, bf16[896,1792]{1,0:T(8,128)(2,1)} %collective-permute-done, bf16[896,1792]{1,0:T(8,128)(2,1)} %collective-permute-done.5, pred[]{:T(512)S(6)} %or.4, ...), kind=kOutput, calls=%fused_computation.12 | convolution fusion | flops 5757796352 | bytes 22478854 | tf_op jit(solution)/shard_map/dot_general | solution.py:66
  319.1 11.8 %fusion.11 = f32[896,1792]{0,1:T(8,128)} fusion(bf16[7168,1792]{1,0:T(8,128)(2,1)} %all-gather.5.cloned.1.call-done, s32[]{:T(128)S(6)} %select_n.140, bf16[896,1792]{1,0:T(8,128)(2,1)} %collective-permute-done.2, bf16[896,1792]{1,0:T(8,128)(2,1)} %collective-permute-done.3, pred[]{:T(512)S(6)} %eq.32), kind=kOutput, calls=%fused_computation.14 | convolution fusion | flops 5756190720 | bytes 19267588 | tf_op jit(solution)/shard_map/dot_general | solution.py:66
  330.9 10.6 %fusion.15 = f32[1792,896]{1,0:T(8,128)} fusion(bf16[896,1792]{1,0:T(8,128)(2,1)S(1)} %copy-done, bf16[7168,1792]{1,0:T(8,128)(2,1)} %all-gather.5.cloned.1.call-done, s32[]{:T(128)S(6)} %select_n.133), kind=kOutput, calls=%fused_computation.18 | convolution fusion | flops 5754585088 | bytes 16056324 | tf_op jit(solution)/shard_map/dot_general | solution.py:66
  341.5 17.5 %collective-permute-done.10 = bf16[896,1792]{1,0:T(8,128)(2,1)} collective-permute-done((bf16[896,1792]{1,0:T(8,128)(2,1)}, bf16[896,1792]{1,0:T(8,128)(2,1)}, u32[]{:S(2)}, u32[]{:S(2)}) %collective-permute-start.10) | collective-permute-done | bytes 3211296 | tf_op jit(solution)/shard_map/ppermute | solution.py:28
  359.1 0.0 collective-permute-done.11
  359.1 12.6 %fusion.3 = f32[896,1792]{0,1:T(8,128)} fusion(bf16[7168,1792]{1,0:T(8,128)(2,1)} %all-gather.5.cloned.1.call-done, s32[]{:T(128)S(6)} %select_n.161, bf16[896,1792]{1,0:T(8,128)(2,1)} %collective-permute-done.10, bf16[896,1792]{1,0:T(8,128)(2,1)} %collective-permute-done.6, bf16[896,1792]{1,0:T(8,128)(2,1)} %collective-permute-done.11, ...), kind=kOutput, calls=%fused_computation.6 | convolution fusion | flops 5759401984 | bytes 25690120 | tf_op jit(solution)/shard_map/dot_general | solution.py:66
  371.7 11.8 %fusion.13 = f32[896,1792]{0,1:T(8,128)} fusion(bf16[7168,1792]{1,0:T(8,128)(2,1)} %all-gather.3.cloned.1.call-done, s32[]{:T(128)S(6)} %select_n.140, bf16[896,1792]{1,0:T(8,128)(2,1)} %collective-permute-done, bf16[896,1792]{1,0:T(8,128)(2,1)} %collective-permute-done.1, pred[]{:T(512)S(6)} %eq.32), kind=kOutput, calls=%fused_computation.16 | convolution fusion | flops 5756190720 | bytes 19267588 | tf_op jit(solution)/shard_map/dot_general | solution.py:66
  383.5 10.7 %fusion.17 = f32[1792,896]{1,0:T(8,128)} fusion(bf16[896,1792]{1,0:T(8,128)(2,1)S(1)} %copy-done.1, bf16[7168,1792]{1,0:T(8,128)(2,1)} %all-gather.3.cloned.1.call-done, s32[]{:T(128)S(6)} %select_n.133), kind=kOutput, calls=%fused_computation.20 | convolution fusion | flops 5754585088 | bytes 16056324 | tf_op jit(solution)/shard_map/dot_general | solution.py:66
  394.2 32.8 %collective-permute-done.8 = bf16[896,1792]{1,0:T(8,128)(2,1)} collective-permute-done((bf16[896,1792]{1,0:T(8,128)(2,1)}, bf16[896,1792]{1,0:T(8,128)(2,1)}, u32[]{:S(2)}, u32[]{:S(2)}) %collective-permute-start.8) | collective-permute-done | bytes 3211296 | tf_op jit(solution)/shard_map/ppermute | solution.py:28
  427.1 0.0 collective-permute-done.9
  427.1 23.2 %fusion.2 = f32[896,1792]{0,1:T(8,128)} fusion(f32[896,1792]{0,1:T(8,128)} %fusion.3, f32[896,1792]{0,1:T(8,128)} %fusion.9, f32[896,1792]{0,1:T(8,128)} %fusion.7, f32[896,1792]{0,1:T(8,128)} %fusion.13, f32[896,1792]{0,1:T(8,128)} %fusion.11, f32[1792,896]{1,0:T(8,128)} %fusion.17, f32[1792,896]{1,0:T(8,128)} %fusion.15, f32[1792]{0:T(1024)S(1)} %sub.15, ...), kind=kOutput, calls=%fused_computation.5 | convolution fusion | flops 5773852672 | bytes 70658568 | tf_op jit(solution)/shard_map/dot_general | solution.py:66
  450.3 7.8 %copy.20 = f32[896,1792]{1,0:T(8,128)} copy(f32[896,1792]{0,1:T(8,128)} %fusion.2) | data formatting | bytes 12845056 | tf_op jit(solution)/shard_map/div | solution.py:79
  (9 shorter events, 0.0 us)
Async XLA Ops:
  6.5 1.9 copy-start
  6.5 152.8 %copy-start.3 = (f32[80]{0:T(128)S(1)}, f32[80]{0:T(128)}, u32[]{:S(2)}) copy-start(f32[80]{0:T(128)} %param.8) | copy-start | bytes 964
  6.5 153.0 %copy-start.2 = (f32[1000]{0:T(1024)S(1)}, f32[1000]{0:T(1024)}, u32[]{:S(2)}) copy-start(f32[1000]{0:T(1024)} %param.9) | copy-start | bytes 12004
  6.5 287.4 %all-gather.5.cloned.1.call-start = ((), (), s32[]{:S(2)}) async-start(), calls=%async_computation.1 | async-start | bytes 28901376 | tf_op jit(solution)/shard_map/all_gather | solution.py:53
  7.3 299.3 %all-gather.3.cloned.1.call-start = ((), (), s32[]{:S(2)}) async-start(), calls=%async_computation | async-start | bytes 28901376 | tf_op jit(solution)/shard_map/all_gather | solution.py:54
  8.4 75.4 %collective-permute-start.2 = (bf16[896,1792]{1,0:T(8,128)(2,1)S(1)}, bf16[896,1792]{1,0:T(8,128)(2,1)}, u32[]{:S(2)}, u32[]{:S(2)}) collective-permute-start(bf16[896,1792]{1,0:T(8,128)(2,1)S(1)} %copy-done), channel_id=1, source_target_pairs={{1,0},{2,1},{3,2},{5,4},{6,5},{7,6},{9,8},{10,9},{11,10},{13,12},{... | collective-permute-start | bytes 9633800 | tf_op jit(solution)/shard_map/ppermute | solution.py:28
  9.7 75.5 %collective-permute-start.3 = (bf16[896,1792]{1,0:T(8,128)(2,1)S(1)}, bf16[896,1792]{1,0:T(8,128)(2,1)}, u32[]{:S(2)}, u32[]{:S(2)}) collective-permute-start(bf16[896,1792]{1,0:T(8,128)(2,1)S(1)} %copy-done), channel_id=1, source_target_pairs={{0,1},{1,2},{2,3},{4,5},{5,6},{6,7},{8,9},{9,10},{10,11},{12,13},{... | collective-permute-start | bytes 9633800 | tf_op jit(solution)/shard_map/ppermute | solution.py:27
  17.0 135.6 %collective-permute-start = (bf16[896,1792]{1,0:T(8,128)(2,1)}, bf16[896,1792]{1,0:T(8,128)(2,1)}, u32[]{:S(2)}, u32[]{:S(2)}) collective-permute-start(bf16[896,1792]{1,0:T(8,128)(2,1)} %param.6), channel_id=1, source_target_pairs={{1,0},{2,1},{3,2},{5,4},{6,5},{7,6},{9,8},{10,9},{11,10},{13,12},{... | collective-permute-start | bytes 9633800 | tf_op jit(solution)/shard_map/ppermute | solution.py:28
  18.3 135.6 %collective-permute-start.1 = (bf16[896,1792]{1,0:T(8,128)(2,1)}, bf16[896,1792]{1,0:T(8,128)(2,1)}, u32[]{:S(2)}, u32[]{:S(2)}) collective-permute-start(bf16[896,1792]{1,0:T(8,128)(2,1)} %param.6), channel_id=1, source_target_pairs={{0,1},{1,2},{2,3},{4,5},{5,6},{6,7},{8,9},{9,10},{10,11},{12,13},{... | collective-permute-start | bytes 9633800 | tf_op jit(solution)/shard_map/ppermute | solution.py:27
  83.8 137.6 %collective-permute-start.6 = (bf16[896,1792]{1,0:T(8,128)(2,1)}, bf16[896,1792]{1,0:T(8,128)(2,1)}, u32[]{:S(2)}, u32[]{:S(2)}) collective-permute-start(bf16[896,1792]{1,0:T(8,128)(2,1)} %collective-permute-done.2), channel_id=1, source_target_pairs={{1,0},{2,1},{5,4},{6,5},{9,8},{10,9},{13,12},{14,13},{17,16},{18,1... | collective-permute-start | bytes 9633800 | tf_op jit(solution)/shard_map/ppermute | solution.py:28
  85.2 137.5 %collective-permute-start.7 = (bf16[896,1792]{1,0:T(8,128)(2,1)}, bf16[896,1792]{1,0:T(8,128)(2,1)}, u32[]{:S(2)}, u32[]{:S(2)}) collective-permute-start(bf16[896,1792]{1,0:T(8,128)(2,1)} %collective-permute-done.3), channel_id=1, source_target_pairs={{1,2},{2,3},{5,6},{6,7},{9,10},{10,11},{13,14},{14,15},{17,18},{18... | collective-permute-start | bytes 9633800 | tf_op jit(solution)/shard_map/ppermute | solution.py:27
  152.6 137.6 %collective-permute-start.4 = (bf16[896,1792]{1,0:T(8,128)(2,1)}, bf16[896,1792]{1,0:T(8,128)(2,1)}, u32[]{:S(2)}, u32[]{:S(2)}) collective-permute-start(bf16[896,1792]{1,0:T(8,128)(2,1)} %collective-permute-done), channel_id=1, source_target_pairs={{1,0},{2,1},{5,4},{6,5},{9,8},{10,9},{13,12},{14,13},{17,16},{18,1... | collective-permute-start | bytes 9633800 | tf_op jit(solution)/shard_map/ppermute | solution.py:28
  153.9 137.6 %collective-permute-start.5 = (bf16[896,1792]{1,0:T(8,128)(2,1)}, bf16[896,1792]{1,0:T(8,128)(2,1)}, u32[]{:S(2)}, u32[]{:S(2)}) collective-permute-start(bf16[896,1792]{1,0:T(8,128)(2,1)} %collective-permute-done.1), channel_id=1, source_target_pairs={{1,2},{2,3},{5,6},{6,7},{9,10},{10,11},{13,14},{14,15},{17,18},{18... | collective-permute-start | bytes 9633800 | tf_op jit(solution)/shard_map/ppermute | solution.py:27
  221.4 137.6 %collective-permute-start.10 = (bf16[896,1792]{1,0:T(8,128)(2,1)}, bf16[896,1792]{1,0:T(8,128)(2,1)}, u32[]{:S(2)}, u32[]{:S(2)}) collective-permute-start(bf16[896,1792]{1,0:T(8,128)(2,1)} %collective-permute-done.6), channel_id=1, source_target_pairs={{1,0},{5,4},{9,8},{13,12},{17,16},{21,20},{25,24},{29,28}} | collective-permute-start | bytes 9633800 | tf_op jit(solution)/shard_map/ppermute | solution.py:28
  222.7 136.3 %collective-permute-start.11 = (bf16[896,1792]{1,0:T(8,128)(2,1)}, bf16[896,1792]{1,0:T(8,128)(2,1)}, u32[]{:S(2)}, u32[]{:S(2)}) collective-permute-start(bf16[896,1792]{1,0:T(8,128)(2,1)} %collective-permute-done.7), channel_id=1, source_target_pairs={{2,3},{6,7},{10,11},{14,15},{18,19},{22,23},{26,27},{30,31}} | collective-permute-start | bytes 9633800 | tf_op jit(solution)/shard_map/ppermute | solution.py:27
  290.2 136.8 %collective-permute-start.8 = (bf16[896,1792]{1,0:T(8,128)(2,1)}, bf16[896,1792]{1,0:T(8,128)(2,1)}, u32[]{:S(2)}, u32[]{:S(2)}) collective-permute-start(bf16[896,1792]{1,0:T(8,128)(2,1)} %collective-permute-done.4), channel_id=1, source_target_pairs={{1,0},{5,4},{9,8},{13,12},{17,16},{21,20},{25,24},{29,28}} | collective-permute-start | bytes 9633800 | tf_op jit(solution)/shard_map/ppermute | solution.py:28
  291.5 135.5 %collective-permute-start.9 = (bf16[896,1792]{1,0:T(8,128)(2,1)}, bf16[896,1792]{1,0:T(8,128)(2,1)}, u32[]{:S(2)}, u32[]{:S(2)}) collective-permute-start(bf16[896,1792]{1,0:T(8,128)(2,1)} %collective-permute-done.5), channel_id=1, source_target_pairs={{2,3},{6,7},{10,11},{14,15},{18,19},{22,23},{26,27},{30,31}} | collective-permute-start | bytes 9633800 | tf_op jit(solution)/shard_map/ppermute | solution.py:27
  371.7 11.8 %copy-start.1 = (bf16[896,1792]{1,0:T(8,128)(2,1)S(1)}, bf16[896,1792]{1,0:T(8,128)(2,1)}, u32[]{:S(2)}) copy-start(bf16[896,1792]{1,0:T(8,128)(2,1)} %param.6) | copy-start | bytes 9633796
Sparse Core Ops, SparseCore 0:
  9.2 130.2 all-gather.4
  141.4 127.5 all-gather.2

commit v2 on v1

--- a/solution.py
+++ b/solution.py
@@ -1,7 +1,12 @@
 import jax
 import jax.numpy as jnp
 from jax import lax
+from jax.experimental import pallas as pl
+from jax.experimental.pallas import tpu as pltpu
 from jax.sharding import PartitionSpec as P
+
+CHUNKS = 14
+MESH = pl.DeviceIdType.MESH
 
 
 def lookup(energies, orbital_index):
@@ -42,6 +47,160 @@
     return picked
 
 
+def relays(n):
+    if n == 4:
+        upward = {(1, 0): 1, (2, 0): 2, (3, 0): 0, (2, 1): 1, (3, 1): 3, (3, 2): 2}
+        downward = {(0, 1): 1, (0, 2): 0, (0, 3): 3, (1, 2): 2, (1, 3): 1, (2, 3): 2}
+        return {**upward, **downward}
+    chosen = {}
+    for i in range(n):
+        for j in range(n):
+            low, high = min(i, j), max(i, j)
+            near = 2 * (high - low) < n or (2 * (high - low) == n and low % 2 == 0)
+            if i != j:
+                chosen[i, j] = low if near else high
+    return chosen
+
+
+def swap_kernel(n, via, handed, product_ref, out_ref, relay_ref, send_sem, relay_sem, hand_sem, out_sem):
+    row, col = lax.axis_index("row"), lax.axis_index("col")
+    chip, core = row // 2, row % 2
+    rows = out_ref.shape[1]
+    step = rows // CHUNKS
+
+    def look(table):
+        value = jnp.int32(0)
+        for (i, j), entry in table.items():
+            value = jnp.where((chip == i) & (col == j), jnp.int32(entry), value)
+        return value
+
+    barrier = pltpu.get_barrier_semaphore()
+
+    def greet(r, c):
+        pl.semaphore_signal(barrier, inc=1, device_id=(r, c), device_id_type=MESH)
+
+    def chunk(c):
+        return pl.ds(pl.multiple_of(c * step, 8), step)
+
+    @pl.when(chip != col)
+    def _():
+        there = look(via)
+        back = look({(i, j): via[j, i] for i, j in via})
+        slot = look({block: handed[l].index(block) for block, l in via.items()})
+        for side in range(2):
+            greet(2 * there + side, there)
+            greet(2 * back + side, back)
+        pl.semaphore_wait(barrier, 4)
+
+        def copies(c):
+            return [
+                pltpu.make_async_remote_copy(
+                    src_ref=product_ref.at[side, chunk(c)],
+                    dst_ref=relay_ref.at[slot, core, chunk(c)],
+                    send_sem=send_sem.at[side, c],
+                    recv_sem=relay_sem.at[slot, core, c],
+                    device_id=(2 * there + side, there),
+                    device_id_type=MESH,
+                )
+                for side in range(2)
+            ]
+
+        def start(c, carry):
+            for copy in copies(c):
+                copy.start()
+            return carry
+
+        lax.fori_loop(0, CHUNKS, start, 0)
+
+        def finish(c, carry):
+            for half in range(2):
+                part = out_ref.at[half, chunk(c)]
+                pltpu.make_async_copy(part, part, out_sem.at[half, c]).wait()
+            for copy in copies(c):
+                copy.wait_send()
+            return carry
+
+        lax.fori_loop(0, CHUNKS, finish, 0)
+
+    for l in range(n):
+        @pl.when((chip == l) & (col == l))
+        def _(l=l):
+            blocks = handed[l]
+            greet(2 * l + 1 - core, l)
+            for i, j in blocks:
+                for side in range(2):
+                    greet(2 * i + side, j)
+                    greet(2 * j + side, i)
+            pl.semaphore_wait(barrier, 1 + 4 * len(blocks))
+
+            across = pltpu.make_async_remote_copy(
+                src_ref=product_ref.at[1 - core],
+                dst_ref=out_ref.at[core],
+                send_sem=send_sem.at[0, 0],
+                recv_sem=out_sem.at[0, 0],
+                device_id=(2 * l + 1 - core, l),
+                device_id_type=MESH,
+            )
+            across.start()
+            kept = pltpu.make_async_copy(product_ref.at[core], out_ref.at[core], send_sem.at[1, 0])
+            kept.start()
+
+            def hand(slot, half, c):
+                i, j = blocks[slot]
+                return pltpu.make_async_remote_copy(
+                    src_ref=relay_ref.at[slot, half, chunk(c)],
+                    dst_ref=out_ref.at[half, chunk(c)],
+                    send_sem=hand_sem.at[slot, half, c],
+                    recv_sem=out_sem.at[half, c],
+                    device_id=(2 * j + core, i),
+                    device_id_type=MESH,
+                )
+
+            def pass_on(c, carry):
+                for slot in range(len(blocks)):
+                    for half in range(2):
+                        part = relay_ref.at[slot, half, chunk(c)]
+                        pltpu.make_async_copy(part, part, relay_sem.at[slot, half, c]).wait()
+                        hand(slot, half, c).start()
+                return carry
+
+            lax.fori_loop(0, CHUNKS, pass_on, 0)
+
+            def finish(c, carry):
+                for slot in range(len(blocks)):
+                    for half in range(2):
+                        hand(slot, half, c).wait_send()
+                return carry
+
+            lax.fori_loop(0, CHUNKS, finish, 0)
+            kept.wait()
+            across.wait()
+
+
+def swap(product, n):
+    via = relays(n)
+    handed = [[block for block in via if via[block] == l] for l in range(n)]
+    slots = max(len(blocks) for blocks in handed)
+    anywhere = pl.BlockSpec(memory_space=pl.ANY)
+    shape = product.shape
+    return pl.pallas_call(
+        lambda *refs: swap_kernel(n, via, handed, *refs),
+        out_shape=(
+            jax.ShapeDtypeStruct(shape, jnp.float32),
+            jax.ShapeDtypeStruct((slots, *shape), jnp.float32),
+        ),
+        in_specs=[anywhere],
+        out_specs=(anywhere, anywhere),
+        scratch_shapes=[
+            pltpu.SemaphoreType.DMA((2, CHUNKS)),
+            pltpu.SemaphoreType.DMA((slots, 2, CHUNKS)),
+            pltpu.SemaphoreType.DMA((slots, 2, CHUNKS)),
+            pltpu.SemaphoreType.DMA((2, CHUNKS)),
+        ],
+        compiler_params=pltpu.CompilerParams(collective_id=0, has_side_effects=True),
+    )(product)[0]
+
+
 def shards_of(cols):
     orders = [arrivals(c, cols) for c in range(cols)]
 
@@ -49,8 +208,6 @@
         tile_rows, tile_cols = amplitudes.shape
         row, col = lax.axis_index("row"), lax.axis_index("col")
         amp_held = chains(amplitudes, cols)
-        int_held = chains(integrals, cols)
-        amp_panel = lax.all_gather(amplitudes, "row", axis=0, tiled=True)
         int_panel = lax.all_gather(integrals, "row", axis=0, tiled=True)
 
         row_occ = lax.dynamic_slice_in_dim(pair_occ, row * tile_rows, tile_rows)
@@ -60,23 +217,20 @@
         row_gap = lookup(occ_energy, row_occ) - lookup(vir_energy, row_vir)
         col_gap = lookup(occ_energy, col_occ) - lookup(vir_energy, col_vir)
 
-        def term(amp, integ, k):
+        def term(amp, k):
             int_block = lax.dynamic_slice_in_dim(int_panel, k * tile_cols, tile_cols)
-            amp_block = lax.dynamic_slice_in_dim(amp_panel, k * tile_cols, tile_cols)
-            return jnp.dot(amp, int_block, preferred_element_type=jnp.float32) + jnp.dot(
-                integ, amp_block, preferred_element_type=jnp.float32
-            )
-
-        total = term(amplitudes, integrals, col)
+            return jnp.dot(amp, int_block, preferred_element_type=jnp.float32)
+
+        total = term(amplitudes, col)
         for slot in range(cols - 1):
             sources = [order[slot] for order in orders]
             k = jnp.zeros((), jnp.int32)
             for c, (direction, hops) in enumerate(sources):
                 k = jnp.where(col == c, c + hops if direction else c - hops, k)
-            total = total + term(
-                choose(amp_held, sources, col), choose(int_held, sources, col), k
-            )
-        return total / (row_gap[:, None] + col_gap[None, :])
+            total = total + term(choose(amp_held, sources, col), k)
+        mirrored = swap(total.T.reshape(2, tile_rows, tile_rows), cols)
+        mirrored = jnp.concatenate((mirrored[0], mirrored[1]), axis=1)
+        return (total + mirrored) / (row_gap[:, None] + col_gap[None, :])
 
     return shards
 

time: 467 us -> 477 us (1.021)
  Pallas kernels: 0 us -> 148 us
  waiting for transfers between devices: 302 us -> 183 us
  matrix products: 106 us -> 46.9 us
  local copies, waits for them, and re-layouts: 11.3 us -> 40.4 us
  other arithmetic: 1.61 us -> 26.7 us
  starting transfers between devices: 30.7 us -> 13.7 us
    ppermute x6 -> x3, waiting for transfers between devices: 300 us -> 115 us  [chains(): lax.ppermute(down, 'col', [(c, c - 1) for c in range(1, cols - hops + 1)])]
    pallas_call x0 -> x1, Pallas kernels: none -> 148 us  [swap(): pl.pallas_call(lambda *refs: swap_kernel(n, via, handed, *refs), out_shap...]
    ppermute x6 -> x3, waiting for transfers between devices: 0.12 us -> 67.6 us  [chains(): lax.ppermute(up, 'col', [(c, c + 1) for c in range(hops - 1, cols - 1)])]
    dot_general x8 -> x4, matrix products: 106 us -> 46.9 us  [term(): return jnp.dot(amp, int_block, preferred_element_type=jnp.float32)]
    dot_general x0 -> x4, local copies, waits for them, and re-layouts: none -> 31.2 us  [term(): return jnp.dot(amp, int_block, preferred_element_type=jnp.float32)]
    ppermute x6 -> x3, starting transfers between devices: 23 us -> 9.84 us  [chains(): lax.ppermute(up, 'col', [(c, c + 1) for c in range(hops - 1, cols - 1)])]
    add x0 -> x1, other arithmetic: none -> 11.8 us  [shards(): total = total + term(choose(amp_held, sources, col), k)]
    div x0 -> x1, other arithmetic: none -> 10.6 us  [shards(): return (total + mirrored) / (row_gap[:, None] + col_gap[None, :])]
  transfers between devices with their start and end apart: 14 -> 7, of which waited for: 7 -> 4; matrix products, arithmetic and copies ran while one was open for 19% -> 6% of each run, Pallas kernels for 0% -> 0%
where the time goes in v2:
time: 477 us; the launch traced here: 472 us
  waiting for transfers between devices  183 us (38%)
  Pallas kernels  148 us (31%)
  matrix products  46.9 us (10%)
  local copies, waits for them, and re-layouts  40.4 us (8%)
  other arithmetic  26.7 us (6%)
  starting transfers between devices  13.7 us (3%)
  between operations  13.6 us (3%)
    pallas_call x1, Pallas kernels, swap(): pl.pallas_call(lambda *refs: swap_kernel(n, via, handed, *refs), out_shap...  148 us
    ppermute x3, waiting for transfers between devices, chains(): lax.ppermute(down, 'col', [(c, c - 1) for c in range(1, cols - hops + 1)])  115 us
    ppermute x3, waiting for transfers between devices, chains(): lax.ppermute(up, 'col', [(c, c + 1) for c in range(hops - 1, cols - 1)])  67.6 us
    dot_general x4, matrix products, term(): return jnp.dot(amp, int_block, preferred_element_type=jnp.float32)  46.9 us
    dot_general x4, local copies, waits for them, and re-layouts, term(): return jnp.dot(amp, int_block, preferred_element_type=jnp.float32)  31.2 us
    add x1, other arithmetic, shards(): total = total + term(choose(amp_held, sources, col), k)  11.8 us
    div x1, other arithmetic, shards(): return (total + mirrored) / (row_gap[:, None] + col_gap[None, :])  10.6 us
    ppermute x3, starting transfers between devices, chains(): lax.ppermute(up, 'col', [(c, c + 1) for c in range(hops - 1, cols - 1)])  9.84 us
  transfers between devices with their start and end apart: 7, of which 4 were waited for; matrix products, arithmetic and copies ran while one was open for 6% of the time, Pallas kernels for 0%

profile of v2, /device:TPU:0, one launch (start us, length us, event | category | flops | bytes accessed | tf_op | source)
XLA Modules:
  0.0 472.1 jit_solution(11216647181978624648)
XLA Ops:
  6.5 0.0 all-gather.2.cloned.1.call-start
  6.5 0.7 all-gather.2.cloned.1.call-update
  7.3 5.1 %collective-permute-start.1 = (bf16[896,1792]{1,0:T(8,128)(2,1)}, bf16[896,1792]{1,0:T(8,128)(2,1)S(1)}, u32[]{:S(2)}, u32[]{:S(2)}) collective-permute-start(bf16[896,1792]{1,0:T(8,128)(2,1)} %param.6), channel_id=1, source_target_pairs={{0,1},{1,2},{2,3},{4,5},{5,6},{6,7},{8,9},{9,10},{10,11},{12,13},{... | collective-permute-start | bytes 9633800 | tf_op jit(solution)/shard_map/ppermute | solution.py:32
  12.4 1.3 collective-permute-start
  13.7 67.6 %collective-permute-done.1 = bf16[896,1792]{1,0:T(8,128)(2,1)S(1)} collective-permute-done((bf16[896,1792]{1,0:T(8,128)(2,1)}, bf16[896,1792]{1,0:T(8,128)(2,1)S(1)}, u32[]{:S(2)}, u32[]{:S(2)}) %collective-permute-start.1) | collective-permute-done | bytes 3211296 | tf_op jit(solution)/shard_map/ppermute | solution.py:32
  81.3 0.0 copy-start
  81.3 1.7 copy-done
  82.9 2.3 collective-permute-start.3
  85.2 0.2 collective-permute-done
  85.5 0.0 copy-start.1
  85.5 1.3 collective-permute-start.2
  86.8 0.0 collective-permute-done.3
  86.8 0.4 copy-done.1
  87.2 2.4 collective-permute-start.5
  89.6 71.3 %collective-permute-done.2 = bf16[896,1792]{1,0:T(8,128)(2,1)} collective-permute-done((bf16[896,1792]{1,0:T(8,128)(2,1)S(1)}, bf16[896,1792]{1,0:T(8,128)(2,1)}, u32[]{:S(2)}, u32[]{:S(2)}) %collective-permute-start.2) | collective-permute-done | bytes 3211296 | tf_op jit(solution)/shard_map/ppermute | solution.py:33
  160.9 1.3 collective-permute-start.4
  162.2 0.8 dynamic_slice.28
  163.0 0.8 dynamic_slice.29
  163.8 0.8 dynamic_slice.30
  164.5 0.8 dynamic_slice.31
  165.3 0.8 select_reduce_fusion.3
  166.1 1.2 select_reduce_fusion.1
  167.3 0.8 select_reduce_fusion.2
  168.1 1.6 select_reduce_fusion
  169.7 0.0 all-gather.2.cloned.1.call-done
  169.7 11.8 %fusion.9 = f32[1792,896]{1,0:T(8,128)} fusion(bf16[896,1792]{1,0:T(8,128)(2,1)} %param.6, bf16[7168,1792]{1,0:T(8,128)(2,1)} %all-gather.2.cloned.1.call-done, s32[]{:T(128)S(6)} %select_n.105), kind=kOutput, calls=%fused_computation.16 | convolution fusion | flops 5754585088 | bytes 16056324 | tf_op jit(solution)/shard_map/dot_general | solution.py:222
  181.5 7.8 %copy.11 = f32[1792,896]{0,1:T(8,128)} copy(f32[1792,896]{1,0:T(8,128)} %fusion.9) | data formatting | bytes 12845056 | tf_op jit(solution)/shard_map/dot_general | solution.py:222
  189.3 0.0 collective-permute-done.5
  189.3 43.4 %collective-permute-done.4 = bf16[896,1792]{1,0:T(8,128)(2,1)} collective-permute-done((bf16[896,1792]{1,0:T(8,128)(2,1)}, bf16[896,1792]{1,0:T(8,128)(2,1)}, u32[]{:S(2)}, u32[]{:S(2)}) %collective-permute-start.4) | collective-permute-done | bytes 3211296 | tf_op jit(solution)/shard_map/ppermute | solution.py:33
  232.6 11.9 %fusion.3 = f32[896,1792]{1,0:T(8,128)} fusion(bf16[7168,1792]{1,0:T(8,128)(2,1)} %all-gather.2.cloned.1.call-done, s32[]{:T(128)S(6)} %select_n.130, bf16[896,1792]{1,0:T(8,128)(2,1)} %collective-permute-done.4, bf16[896,1792]{1,0:T(8,128)(2,1)} %collective-permute-done.2, bf16[896,1792]{1,0:T(8,128)(2,1)} %collective-permute-done.5, ...), kind=kOutput, calls=%fused_computation.10 | convolution fusion | flops 5759401984 | bytes 25690120 | tf_op jit(solution)/shard_map/dot_general | solution.py:222
  244.5 7.8 %copy.14 = f32[896,1792]{0,1:T(8,128)} copy(f32[896,1792]{1,0:T(8,128)} %fusion.3) | data formatting | bytes 12845056 | tf_op jit(solution)/shard_map/dot_general | solution.py:222
  252.3 12.0 %fusion.5 = f32[896,1792]{1,0:T(8,128)} fusion(bf16[7168,1792]{1,0:T(8,128)(2,1)} %all-gather.2.cloned.1.call-done, s32[]{:T(128)S(6)} %select_n.120, bf16[896,1792]{1,0:T(8,128)(2,1)} %collective-permute-done.2, bf16[896,1792]{1,0:T(8,128)(2,1)} %copy-done.1, bf16[896,1792]{1,0:T(8,128)(2,1)} %collective-permute-done.3, pred[]{:T(512)S(6)} %or.3, pred[]{:T(512)S(6)} %eq.32), kind=kOutput, calls=%fused_computation.12 | convolution fusion | flops 5757796352 | bytes 22478854 | tf_op jit(solution)/shard_map/dot_general | solution.py:222
  264.3 7.8 %copy.13 = f32[896,1792]{0,1:T(8,128)} copy(f32[896,1792]{1,0:T(8,128)} %fusion.5) | data formatting | bytes 12845056 | tf_op jit(solution)/shard_map/dot_general | solution.py:222
  272.1 11.3 %fusion.7 = f32[896,1792]{1,0:T(8,128)} fusion(bf16[7168,1792]{1,0:T(8,128)(2,1)} %all-gather.2.cloned.1.call-done, s32[]{:T(128)S(6)} %select_n.112, bf16[896,1792]{1,0:T(8,128)(2,1)} %copy-done.1, bf16[896,1792]{1,0:T(8,128)(2,1)} %copy-done, pred[]{:T(512)S(6)} %eq.32), kind=kOutput, calls=%fused_computation.14 | convolution fusion | flops 5756190720 | bytes 19267588 | tf_op jit(solution)/shard_map/dot_general | solution.py:222
  283.4 7.8 %copy.12 = f32[896,1792]{0,1:T(8,128)} copy(f32[896,1792]{1,0:T(8,128)} %fusion.7) | data formatting | bytes 12845056 | tf_op jit(solution)/shard_map/dot_general | solution.py:222
  291.2 11.8 %bitcast_add_fusion = f32[1792,896]{1,0:T(8,128)} fusion(f32[896,1792]{0,1:T(8,128)} %copy.14, f32[896,1792]{0,1:T(8,128)} %copy.13, f32[1792,896]{1,0:T(8,128)} %fusion.9, f32[896,1792]{0,1:T(8,128)} %copy.12), kind=kLoop, calls=%fused_computation.4 | loop fusion | flops 4816896 | bytes 32112640 | tf_op jit(solution)/shard_map/add | solution.py:230
  303.0 0.0 slice-start
  303.0 147.5 %shard_map.64 = (f32[2,896,896]{2,1,0:T(8,128)}, f32[4,2,896,896]{3,2,1,0:T(8,128)}) custom-call(f32[2,896,896]{2,1,0:T(8,128)} %bitcast.26), custom_call_target="tpu_custom_call" | custom-call | tf_op jit(solution)/shard_map/pallas_call | solution.py:186
  450.5 0.0 slice-start.1
  450.5 3.4 slice_bitcast_fusion.1
  454.0 0.0 slice-done
  454.0 0.6 slice-done.1
  454.6 10.6 %fusion = f32[896,1792]{1,0:T(8,128)} fusion(f32[896,896]{1,0:T(8,128)S(1)} %get-tuple-element.8, f32[896,896]{1,0:T(8,128)S(1)} %get-tuple-element.7, f32[896,1792]{1,0:T(8,128)} %fusion.3, f32[896,1792]{1,0:T(8,128)} %fusion.5, f32[896,1792]{1,0:T(8,128)} %fusion.7, f32[1792,896]{0,1:T(8,128)S(1)} %bitcast.25, f32[1792]{0:T(1024)S(1)} %sub.15, f32[896]{0:T(1024)S(1)} %sub.14), kind=kLoop, calls=%fused_computation.3 | loop fusion | flops 11239424 | bytes 38545920 | tf_op jit(solution)/shard_map/div | solution.py:233
  (3 shorter events, 0.0 us)
Async XLA Ops:
  6.5 163.2 %all-gather.2.cloned.1.call-start = ((), (), s32[]{:S(2)}) async-start(), calls=%async_computation | async-start | bytes 28901376 | tf_op jit(solution)/shard_map/all_gather | solution.py:211
  7.3 74.0 %collective-permute-start.1 = (bf16[896,1792]{1,0:T(8,128)(2,1)}, bf16[896,1792]{1,0:T(8,128)(2,1)S(1)}, u32[]{:S(2)}, u32[]{:S(2)}) collective-permute-start(bf16[896,1792]{1,0:T(8,128)(2,1)} %param.6), channel_id=1, source_target_pairs={{0,1},{1,2},{2,3},{4,5},{5,6},{6,7},{8,9},{9,10},{10,11},{12,13},{... | collective-permute-start | bytes 9633800 | tf_op jit(solution)/shard_map/ppermute | solution.py:32
  12.4 73.1 %collective-permute-start = (bf16[896,1792]{1,0:T(8,128)(2,1)}, bf16[896,1792]{1,0:T(8,128)(2,1)S(1)}, u32[]{:S(2)}, u32[]{:S(2)}) collective-permute-start(bf16[896,1792]{1,0:T(8,128)(2,1)} %param.6), channel_id=1, source_target_pairs={{1,0},{2,1},{3,2},{5,4},{6,5},{7,6},{9,8},{10,9},{11,10},{13,12},{... | collective-permute-start | bytes 9633800 | tf_op jit(solution)/shard_map/ppermute | solution.py:33
  81.3 1.7 copy-start
  82.9 3.8 collective-permute-start.3
  85.5 1.7 copy-start.1
  85.5 75.4 %collective-permute-start.2 = (bf16[896,1792]{1,0:T(8,128)(2,1)S(1)}, bf16[896,1792]{1,0:T(8,128)(2,1)}, u32[]{:S(2)}, u32[]{:S(2)}) collective-permute-start(bf16[896,1792]{1,0:T(8,128)(2,1)S(1)} %collective-permute-done), channel_id=1, source_target_pairs={{1,0},{2,1},{5,4},{6,5},{9,8},{10,9},{13,12},{14,13},{17,16},{18,1... | collective-permute-start | bytes 9633800 | tf_op jit(solution)/shard_map/ppermute | solution.py:33
  87.2 102.1 %collective-permute-start.5 = (bf16[896,1792]{1,0:T(8,128)(2,1)}, bf16[896,1792]{1,0:T(8,128)(2,1)}, u32[]{:S(2)}, u32[]{:S(2)}) collective-permute-start(bf16[896,1792]{1,0:T(8,128)(2,1)} %collective-permute-done.3), channel_id=1, source_target_pairs={{2,3},{6,7},{10,11},{14,15},{18,19},{22,23},{26,27},{30,31}} | collective-permute-start | bytes 9633800 | tf_op jit(solution)/shard_map/ppermute | solution.py:32
  160.9 71.8 %collective-permute-start.4 = (bf16[896,1792]{1,0:T(8,128)(2,1)}, bf16[896,1792]{1,0:T(8,128)(2,1)}, u32[]{:S(2)}, u32[]{:S(2)}) collective-permute-start(bf16[896,1792]{1,0:T(8,128)(2,1)} %collective-permute-done.2), channel_id=1, source_target_pairs={{1,0},{5,4},{9,8},{13,12},{17,16},{21,20},{25,24},{29,28}} | collective-permute-start | bytes 9633800 | tf_op jit(solution)/shard_map/ppermute | solution.py:33
  303.0 151.0 %slice-start = ((s8[6422528]{0:T(1024)(128)(4,1)}), s8[2228224]{0:T(1024)(128)(4,1)S(1)}, s32[]{:S(2)}) async-start(s8[6422528]{0:T(1024)(128)(4,1)} %bitcast.24), calls=%async_computation.1 | async-start | bytes 4456448
  450.5 4.1 slice-start.1
Sparse Core Ops, SparseCore 0:
  9.2 130.2 all-gather.1

commit v3 on v2

--- a/solution.py
+++ b/solution.py
@@ -227,7 +227,9 @@
             k = jnp.zeros((), jnp.int32)
             for c, (direction, hops) in enumerate(sources):
                 k = jnp.where(col == c, c + hops if direction else c - hops, k)
+            total = lax.optimization_barrier(total)
             total = total + term(choose(amp_held, sources, col), k)
+        total = lax.optimization_barrier(total)
         mirrored = swap(total.T.reshape(2, tile_rows, tile_rows), cols)
         mirrored = jnp.concatenate((mirrored[0], mirrored[1]), axis=1)
         return (total + mirrored) / (row_gap[:, None] + col_gap[None, :])

time: 477 us -> 419 us (0.88)
  local copies, waits for them, and re-layouts: 40.4 us -> 15.7 us
  other arithmetic: 26.7 us -> 7.72 us
  waiting for transfers between devices: 183 us -> 167 us
  matrix products: 46.9 us -> 41.7 us
  Pallas kernels: 148 us -> 153 us
    ppermute x3, waiting for transfers between devices: 67.6 us -> 0.01 us  [chains(): lax.ppermute(up, 'col', [(c, c + 1) for c in range(hops - 1, cols - 1)])]
    ppermute x3, waiting for transfers between devices: 115 us -> 166 us  [chains(): lax.ppermute(down, 'col', [(c, c - 1) for c in range(1, cols - hops + 1)])]
    dot_general x4 -> x0, local copies, waits for them, and re-layouts: 31.2 us -> none  [term(): return jnp.dot(amp, int_block, preferred_element_type=jnp.float32)]
    add x1 -> x0, other arithmetic: 11.8 us -> none  [shards(): total = total + term(choose(amp_held, sources, col), k)]
    transpose x0 -> x1, local copies, waits for them, and re-layouts: none -> 7.79 us  [shards(): mirrored = swap(total.T.reshape(2, tile_rows, tile_rows), cols)]
    div x1, other arithmetic: 10.6 us -> 3.42 us  [shards(): return (total + mirrored) / (row_gap[:, None] + col_gap[None, :])]
    pallas_call x1, Pallas kernels: 148 us -> 153 us  [swap(): pl.pallas_call(lambda *refs: swap_kernel(n, via, handed, *refs), out_shap...]
    dot_general x4, matrix products: 46.9 us -> 41.7 us  [term(): return jnp.dot(amp, int_block, preferred_element_type=jnp.float32)]
  transfers between devices with their start and end apart: 7 -> 7, of which waited for: 4 -> 3; matrix products, arithmetic and copies ran while one was open for 6% -> 9% of each run, Pallas kernels for 0% -> 0%
where the time goes in v3:
time: 419 us; the launch traced here: 415 us
  waiting for transfers between devices  167 us (40%)
  Pallas kernels  153 us (37%)
  matrix products  41.7 us (10%)
  starting transfers between devices  15.8 us (4%)
  local copies, waits for them, and re-layouts  15.7 us (4%)
  between operations  13.5 us (3%)
  other arithmetic  7.72 us (2%)
    ppermute x3, waiting for transfers between devices, chains(): lax.ppermute(down, 'col', [(c, c - 1) for c in range(1, cols - hops + 1)])  166 us
    pallas_call x1, Pallas kernels, swap(): pl.pallas_call(lambda *refs: swap_kernel(n, via, handed, *refs), out_shap...  153 us
    dot_general x4, matrix products, term(): return jnp.dot(amp, int_block, preferred_element_type=jnp.float32)  41.7 us
    ppermute x3, starting transfers between devices, chains(): lax.ppermute(up, 'col', [(c, c + 1) for c in range(hops - 1, cols - 1)])  12 us
  transfers between devices with their start and end apart: 7, of which 3 were waited for; matrix products, arithmetic and copies ran while one was open for 9% of the time, Pallas kernels for 0%

profile of v3, /device:TPU:0, one launch (start us, length us, event | category | flops | bytes accessed | tf_op | source)
XLA Modules:
  0.0 414.6 jit_solution(8990622615930257123)
XLA Ops:
  6.5 0.0 all-gather.2.cloned.1.call-start
  6.5 0.7 all-gather.2.cloned.1.call-update
  7.3 1.3 collective-permute-start
  8.6 7.2 %collective-permute-start.1 = (bf16[896,1792]{1,0:T(8,128)(2,1)}, bf16[896,1792]{1,0:T(8,128)(2,1)}, u32[]{:S(2)}, u32[]{:S(2)}) collective-permute-start(bf16[896,1792]{1,0:T(8,128)(2,1)} %param.6), channel_id=1, source_target_pairs={{0,1},{1,2},{2,3},{4,5},{5,6},{6,7},{8,9},{9,10},{10,11},{12,13},{... | collective-permute-start | bytes 9633800 | tf_op jit(solution)/shard_map/ppermute | solution.py:32
  15.8 66.2 %collective-permute-done = bf16[896,1792]{1,0:T(8,128)(2,1)} collective-permute-done((bf16[896,1792]{1,0:T(8,128)(2,1)}, bf16[896,1792]{1,0:T(8,128)(2,1)}, u32[]{:S(2)}, u32[]{:S(2)}) %collective-permute-start) | collective-permute-done | bytes 3211296 | tf_op jit(solution)/shard_map/ppermute | solution.py:33
  82.0 1.3 collective-permute-start.2
  83.3 0.0 collective-permute-done.1
  83.3 2.4 collective-permute-start.3
  85.7 0.8 dynamic_slice.31
  86.5 0.8 dynamic_slice.30
  87.2 0.8 dynamic_slice.29
  88.0 0.8 dynamic_slice.28
  88.8 0.8 select_reduce_fusion.2
  89.6 1.6 select_reduce_fusion
  91.2 0.8 select_reduce_fusion.3
  91.9 1.2 select_reduce_fusion.1
  93.1 61.7 %collective-permute-done.2 = bf16[896,1792]{1,0:T(8,128)(2,1)S(1)} collective-permute-done((bf16[896,1792]{1,0:T(8,128)(2,1)}, bf16[896,1792]{1,0:T(8,128)(2,1)S(1)}, u32[]{:S(2)}, u32[]{:S(2)}) %collective-permute-start.2) | collective-permute-done | bytes 3211296 | tf_op jit(solution)/shard_map/ppermute | solution.py:33
  154.8 1.3 collective-permute-start.4
  156.1 0.0 collective-permute-done.3
  156.1 2.4 collective-permute-start.5
  158.5 0.0 all-gather.2.cloned.1.call-done
  158.5 9.8 %fusion.9 = f32[896,1792]{1,0:T(8,128)S(1)} fusion(bf16[896,1792]{1,0:T(8,128)(2,1)} %param.6, bf16[7168,1792]{1,0:T(8,128)(2,1)} %all-gather.2.cloned.1.call-done, s32[]{:T(128)S(6)} %select_n.105), kind=kOutput, calls=%fused_computation.12 | convolution fusion | flops 5754585088 | bytes 16056324 | tf_op jit(solution)/shard_map/dot_general | solution.py:222
  168.3 9.8 %fusion.12 = f32[896,1792]{1,0:T(8,128)S(1)} fusion(f32[896,1792]{1,0:T(8,128)S(1)} %fusion.9, bf16[7168,1792]{1,0:T(8,128)(2,1)} %all-gather.2.cloned.1.call-done, s32[]{:T(128)S(6)} %select_n.112, bf16[896,1792]{1,0:T(8,128)(2,1)} %collective-permute-done, bf16[896,1792]{1,0:T(8,128)(2,1)} %collective-permute-done.1, pred[]{:T(512)S(6)} %eq.32), kind=kOutput, calls=%fused_computation.13 | convolution fusion | flops 5757796352 | bytes 25690116 | tf_op jit(solution)/shard_map/dot_general | solution.py:222
  178.0 10.0 %fusion.15 = f32[896,1792]{1,0:T(8,128)S(1)} fusion(f32[896,1792]{1,0:T(8,128)S(1)} %fusion.12, bf16[7168,1792]{1,0:T(8,128)(2,1)} %all-gather.2.cloned.1.call-done, s32[]{:T(128)S(6)} %select_n.120, bf16[896,1792]{1,0:T(8,128)(2,1)S(1)} %collective-permute-done.2, bf16[896,1792]{1,0:T(8,128)(2,1)} %collective-permute-done, ...), kind=kOutput, calls=%fused_computation.14 | convolution fusion | flops 5759401984 | bytes 28901382 | tf_op jit(solution)/shard_map/dot_general | solution.py:222
  188.1 38.5 %collective-permute-done.4 = bf16[896,1792]{1,0:T(8,128)(2,1)} collective-permute-done((bf16[896,1792]{1,0:T(8,128)(2,1)S(1)}, bf16[896,1792]{1,0:T(8,128)(2,1)}, u32[]{:S(2)}, u32[]{:S(2)}) %collective-permute-start.4) | collective-permute-done | bytes 3211296 | tf_op jit(solution)/shard_map/ppermute | solution.py:33
  226.5 0.0 collective-permute-done.5
  226.6 12.1 %fusion.18 = f32[896,1792]{1,0:T(8,128)} fusion(f32[896,1792]{1,0:T(8,128)S(1)} %fusion.15, bf16[7168,1792]{1,0:T(8,128)(2,1)} %all-gather.2.cloned.1.call-done, s32[]{:T(128)S(6)} %select_n.130, bf16[896,1792]{1,0:T(8,128)(2,1)} %collective-permute-done.4, bf16[896,1792]{1,0:T(8,128)(2,1)S(1)} %collective-permute-done.2, ...), kind=kOutput, calls=%fused_computation.15 | convolution fusion | flops 5761007616 | bytes 32112648 | tf_op jit(solution)/shard_map/dot_general | solution.py:222
  238.7 7.8 %copy.10 = f32[1792,896]{1,0:T(8,128)} copy(f32[1792,896]{0,1:T(8,128)} %bitcast.9) | data formatting | bytes 12845056 | tf_op jit(solution)/shard_map/transpose | solution.py:233
  246.5 153.1 %shard_map.64 = (f32[2,896,896]{2,1,0:T(8,128)}, f32[4,2,896,896]{3,2,1,0:T(8,128)}) custom-call(f32[2,896,896]{2,1,0:T(8,128)} %bitcast.12), custom_call_target="tpu_custom_call" | custom-call | tf_op jit(solution)/shard_map/pallas_call | solution.py:186
  399.6 0.0 slice-start
  399.6 0.0 slice-start.1
  399.6 3.4 slice_bitcast_fusion.1
  403.0 0.6 slice-done
  403.7 0.7 slice-done.1
  404.4 3.4 fusion
  (3 shorter events, 0.0 us)
Async XLA Ops:
  6.5 152.0 %all-gather.2.cloned.1.call-start = ((), (), s32[]{:S(2)}) async-start(), calls=%async_computation | async-start | bytes 28901376 | tf_op jit(solution)/shard_map/all_gather | solution.py:211
  7.3 74.7 %collective-permute-start = (bf16[896,1792]{1,0:T(8,128)(2,1)}, bf16[896,1792]{1,0:T(8,128)(2,1)}, u32[]{:S(2)}, u32[]{:S(2)}) collective-permute-start(bf16[896,1792]{1,0:T(8,128)(2,1)} %param.6), channel_id=1, source_target_pairs={{1,0},{2,1},{3,2},{5,4},{6,5},{7,6},{9,8},{10,9},{11,10},{13,12},{... | collective-permute-start | bytes 9633800 | tf_op jit(solution)/shard_map/ppermute | solution.py:33
  8.6 74.7 %collective-permute-start.1 = (bf16[896,1792]{1,0:T(8,128)(2,1)}, bf16[896,1792]{1,0:T(8,128)(2,1)}, u32[]{:S(2)}, u32[]{:S(2)}) collective-permute-start(bf16[896,1792]{1,0:T(8,128)(2,1)} %param.6), channel_id=1, source_target_pairs={{0,1},{1,2},{2,3},{4,5},{5,6},{6,7},{8,9},{9,10},{10,11},{12,13},{... | collective-permute-start | bytes 9633800 | tf_op jit(solution)/shard_map/ppermute | solution.py:32
  82.0 72.8 %collective-permute-start.2 = (bf16[896,1792]{1,0:T(8,128)(2,1)}, bf16[896,1792]{1,0:T(8,128)(2,1)S(1)}, u32[]{:S(2)}, u32[]{:S(2)}) collective-permute-start(bf16[896,1792]{1,0:T(8,128)(2,1)} %collective-permute-done), channel_id=1, source_target_pairs={{1,0},{2,1},{5,4},{6,5},{9,8},{10,9},{13,12},{14,13},{17,16},{18,1... | collective-permute-start | bytes 9633800 | tf_op jit(solution)/shard_map/ppermute | solution.py:33
  83.3 72.8 %collective-permute-start.3 = (bf16[896,1792]{1,0:T(8,128)(2,1)}, bf16[896,1792]{1,0:T(8,128)(2,1)}, u32[]{:S(2)}, u32[]{:S(2)}) collective-permute-start(bf16[896,1792]{1,0:T(8,128)(2,1)} %collective-permute-done.1), channel_id=1, source_target_pairs={{1,2},{2,3},{5,6},{6,7},{9,10},{10,11},{13,14},{14,15},{17,18},{18... | collective-permute-start | bytes 9633800 | tf_op jit(solution)/shard_map/ppermute | solution.py:32
  154.8 71.8 %collective-permute-start.4 = (bf16[896,1792]{1,0:T(8,128)(2,1)S(1)}, bf16[896,1792]{1,0:T(8,128)(2,1)}, u32[]{:S(2)}, u32[]{:S(2)}) collective-permute-start(bf16[896,1792]{1,0:T(8,128)(2,1)S(1)} %collective-permute-done.2), channel_id=1, source_target_pairs={{1,0},{5,4},{9,8},{13,12},{17,16},{21,20},{25,24},{29,28}} | collective-permute-start | bytes 9633800 | tf_op jit(solution)/shard_map/ppermute | solution.py:33
  156.1 70.5 %collective-permute-start.5 = (bf16[896,1792]{1,0:T(8,128)(2,1)}, bf16[896,1792]{1,0:T(8,128)(2,1)}, u32[]{:S(2)}, u32[]{:S(2)}) collective-permute-start(bf16[896,1792]{1,0:T(8,128)(2,1)} %collective-permute-done.3), channel_id=1, source_target_pairs={{2,3},{6,7},{10,11},{14,15},{18,19},{22,23},{26,27},{30,31}} | collective-permute-start | bytes 9633800 | tf_op jit(solution)/shard_map/ppermute | solution.py:32
  399.6 4.1 slice-start
  399.6 4.8 %slice-start.1 = ((s8[6422528]{0:T(1024)(128)(4,1)}), s8[2228224]{0:T(1024)(128)(4,1)S(1)}, s32[]{:S(2)}) async-start(s8[6422528]{0:T(1024)(128)(4,1)} %bitcast.10), calls=%async_computation.2 | async-start | bytes 4456448
Sparse Core Ops, SparseCore 0:
  9.2 130.2 all-gather.1
